TPU v7x, 32 devices: a whole 2x2x4 slice. The times are simulated.
32 devices in a mesh: branch: 2 (over y), ctx: 8 (over z, x), tp: 2 (over core).
Axes of the slice: x: 2, y: 2, z: 4, core: 2. Of those that a mesh axis runs over, the one named last changes fastest.
Arguments:
- queries: bfloat16 [2, 2048, 8192], P('branch', 'ctx', 'tp'), may hold values from -12 to 12
- keys: bfloat16 [2, 2048, 1024], P('branch', 'ctx', 'tp'), may hold values from -12 to 12
- values: bfloat16 [2, 2048, 1024], P('branch', 'ctx', 'tp'), may hold values from -800 to 800
- segments: int32 [2048], replicated, may hold values from 0 to 3, never falling along the last dimension, each value on 1 to 1024 neighbouring positions
- norm_gain: float32 [2, 8192], P('branch', 'tp'), may hold values from 0.5 to 1.5
- head_weight: float32 [2, 8192], P('branch', 'tp'), may hold values from -0.0625 to 0.0625
Outputs:
- normed: bfloat16 [2, 2048, 8192], P('branch', 'ctx', 'tp')
- joined: float32 [2048], P('ctx')
Inputs may be any that keep to these rules, and one draw needn't show every extreme that they name: `segments`: rollout ids never fall along the sequence; each rollout holds 1 to 1024 tokens, and one holds exactly 1024.
All inputs are finite; a program needn't handle non-finite values.
Results may differ from a plain program's by a relative error of at most 0.007.
Values may be sent and summed in bfloat16 or wider, within the bound.
A program may use at most 64 MiB of HBM per device.

v0:
```python
import math

import jax
import jax.numpy as jnp
from jax import lax
from jax.sharding import PartitionSpec as P

H = 64
KVH = 8
HD = 128
D = 8192


NEGATIVE = -1e30
EPSILON = 1e-06


def shifted(block, axis, distance):
    devices = range(lax.axis_size(axis))
    route = [(i - distance, i) for i in devices if i - distance in devices]
    return lax.ppermute(block, axis, route)


def local(queries, keys, values, segments, norm_gain, head_weight):
    rows_dev = queries.shape[1]
    key_columns = keys.shape[2]
    key_heads = key_columns // HD
    per_group = H // KVH
    logit_scale = 1.0 / math.sqrt(HD)
    query_rows = queries[0].reshape(rows_dev, key_heads, per_group, HD)
    first_row = lax.axis_index("ctx") * rows_dev
    position = first_row + jnp.arange(rows_dev, dtype=jnp.int32)
    seg_query = lax.dynamic_slice_in_dim(segments, first_row, rows_dev, 0)
    key_value = jnp.stack([keys[0], values[0]])

    def absorb(running_state, key_block, offset):
        maxima, totals, accumulated = running_state
        key_count = key_block.shape[1]
        key_pos = offset + jnp.arange(key_count, dtype=jnp.int32)
        seg_key = lax.dynamic_slice_in_dim(segments, jnp.maximum(offset, 0), key_count, 0)
        key_rows = key_block[0].reshape(key_count, key_heads, HD)
        value_rows = key_block[1].reshape(key_count, key_heads, HD)
        scores = (
            jnp.einsum("tkgd,pkd->kgtp", query_rows, key_rows, preferred_element_type=jnp.float32)
            * logit_scale
        )
        allowed = (
            (seg_key[None, :] == seg_query[:, None])
            & (key_pos[None, :] <= position[:, None])
            & (key_pos[None, :] >= 0)
        )
        scores = jnp.where(allowed, scores, NEGATIVE)
        new_best = jnp.maximum(maxima, jnp.max(scores, axis=-1))
        rescale = jnp.exp(maxima - new_best)
        weights = jnp.where(allowed, jnp.exp(scores - new_best[..., None]), 0.0)
        totals = totals * rescale + jnp.sum(weights, axis=-1)
        mixed_values = jnp.einsum(
            "kgtp,pkd->kgtd",
            weights.astype(jnp.bfloat16),
            value_rows,
            preferred_element_type=jnp.float32,
        )
        accumulated = accumulated * rescale[..., None] + mixed_values
        return (new_best, totals, accumulated)

    def visit(running_state, key_block, offset):
        return absorb(running_state, key_block, offset)

    initial = (
        jnp.full((key_heads, per_group, rows_dev), NEGATIVE, jnp.float32),
        jnp.zeros((key_heads, per_group, rows_dev), jnp.float32),
        jnp.zeros((key_heads, per_group, rows_dev, HD), jnp.float32),
    )
    span_count = lax.axis_size("ctx") // 2
    start_state = visit(initial, key_value, first_row)

    def step_back(distance, carry):
        state_now, moving = carry
        moved = shifted(moving, "ctx", 1)
        state_now = visit(state_now, moved, first_row - distance * rows_dev)
        return (state_now, moved)

    running_state, unused_block = lax.fori_loop(
        1, span_count + 1, step_back, (start_state, key_value)
    )
    maxima, totals, accumulated = running_state
    outcome = accumulated / totals[..., None]
    outcome = jnp.transpose(outcome, (2, 0, 1, 3)).reshape(rows_dev, key_heads * per_group * HD)
    attended = lax.optimization_barrier(outcome.astype(jnp.bfloat16)).astype(jnp.float32)
    gain_row = norm_gain[0]
    weight_row = head_weight[0]
    squares = jnp.sum(attended * attended, axis=-1)
    square_sum = lax.psum(squares, "tp")
    inverse = lax.rsqrt(square_sum / D + EPSILON)
    partial_value = jnp.sum(attended * inverse[:, None] * gain_row * weight_row, axis=-1)
    row_score = lax.psum(partial_value, "tp")
    normed = (attended * inverse[:, None] * gain_row).astype(jnp.bfloat16)[None]
    joined = lax.psum(row_score, "branch")
    return (normed, joined)


def solution(mesh):
    return jax.shard_map(
        local,
        mesh=mesh,
        in_specs=(
            P("branch", "ctx", "tp"),
            P("branch", "ctx", "tp"),
            P("branch", "ctx", "tp"),
            P(),
            P("branch", "tp"),
            P("branch", "tp"),
        ),
        out_specs=(P("branch", "ctx", "tp"), P("ctx")),
        check_vma=False,
    )
```

profile of v0, /device:TPU:25, one launch (start us, length us, event | category | flops | bytes accessed | tf_op | source)
XLA Modules:
  0.0 138.8 jit_solution(3488914854876130375)
XLA Ops:
  6.0 4.1 %copy.16 = bf16[1,256,4096]{1,2,0:T(8,128)(2,1)} copy(bf16[1,256,4096]{2,1,0:T(8,128)(2,1)} %param.8) | data formatting | bytes 4194304 | tf_op args[0]
  10.0 3.0 %copy.23 = bf16[256,4,8,128]{3,0,2,1:T(8,128)(2,1)S(1)} copy(bf16[256,4,8,128]{0,3,2,1:T(8,128)(2,1)} %bitcast.73) | data formatting | bytes 4194304
  13.1 3.1 %fusion.17 = (f32[4,8,256]{2,1,0:T(8,128)S(1)}, f32[4,256,256,8]{2,1,3,0:T(8,128)S(1)}) fusion(pred[256,256]{0,1:T(8,128)(4,1)S(1)} %and_and_fusion.1, bf16[256,4,8,128]{0,3,2,1:T(8,128)(2,1)} %bitcast.74, bf16[256,4,128,1]{2,1,0,3:T(4,128)(2,1)S(1)} %bitcast.77), kind=kOutput, calls=%fused_computation.24 | convolution fusion | flops 543154176 | bytes 10846208 | tf_op jit(solution)/shard_map/tkgd,pkd->kgtp/dot_general | solution.py:44
  16.2 2.1 %fusion.19 = f32[4,8,256]{2,1,0:T(8,128)S(1)} fusion(f32[4,256,256,8]{2,1,3,0:T(8,128)S(1)} %get-tuple-element.261, f32[4,8,256]{2,1,0:T(8,128)S(1)} %broadcast_maximum_fusion, pred[256,256]{0,1:T(8,128)(4,1)S(1)} %and_and_fusion.1), kind=kLoop, calls=%fused_computation.26 | loop fusion | flops 10477568 | bytes 8519680 | tf_op jit(solution)/shard_map/reduce_sum | solution.py:56
  18.3 4.7 %broadcast_add_fusion = f32[4,8,256,128]{3,2,1,0:T(8,128)} fusion(f32[4,8,256]{2,1,0:T(8,128)S(1)} %get-tuple-element.256, f32[4,256,256,8]{2,1,3,0:T(8,128)S(1)} %get-tuple-element.261, f32[4,8,256]{2,1,0:T(8,128)S(1)} %broadcast_maximum_fusion, pred[256,256]{0,1:T(8,128)(4,1)S(1)} %and_and_fusion.1, bf16[256,4,128,1]{2,1,0,3:T(4,128)(2,1)S(1)} %bitcast.78), kind=kOutput, calls=%fused_computation.43 | convolution fusion | flops 548405248 | bytes 12976128 | tf_op jit(solution)/shard_map/kgtp,pkd->kgtd/dot_general | solution.py:57
  23.0 94.5 %while.21 = (s32[]{:T(128)}, f32[4,8,256]{2,1,0:T(8,128)S(1)}, f32[4,8,256]{2,1,0:T(8,128)S(1)}, f32[4,8,256,128]{3,2,1,0:T(8,128)}, bf16[2,256,512]{1,2,0:T(8,1...) while((s32[]{:T(128)}, f32[4,8,256]{2,1,0:T(8,128)S(1)}, ...), condition=%wide.region_5.6_spmd.clone.clone, body=%wide.region_2.5_spmd.clone.clone.sunk | while | flops 1103381504 | bytes 74720008 | solution.py:83
  23.0 3.1 %collective-permute-start = (bf16[2,256,512]{1,2,0:T(8,128)(2,1)S(1)}, bf16[2,256,512]{1,2,0:T(8,128)(2,1)S(1)}, u32[]{:S(2)}, u32[]{:S(2)}) collective-permute-start(bf16[2,256,512]{1,2,0:T(8,128)(2,1)S(1)} %get-tuple-element.350), channel_id=1, source_target_pairs={{0,2},{2,4},{4,6},{6,8},{8,10},{10,12},{12,14},{1,3},{3,5},{5,7},{... | collective-permute-start | bytes 1572872 | tf_op jit(solution)/shard_map/while/body/eval_jaxpr/ppermute | solution.py:21
  27.1 11.5 %collective-permute-done = bf16[2,256,512]{1,2,0:T(8,128)(2,1)S(1)} collective-permute-done((bf16[2,256,512]{1,2,0:T(8,128)(2,1)S(1)}, bf16[2,256,512]{1,2,0:T(8,128)(2,1)S(1)}, u32[]{:S(2)}, u32[]{:S(2)}) %collective-permute-start) | collective-permute-done | bytes 524320 | tf_op jit(solution)/shard_map/while/body/eval_jaxpr/ppermute | solution.py:21
  40.2 2.1 %fusion.62 = f32[4,8,256]{2,1,0:T(8,128)S(1)} fusion(f32[4,256,256,8]{2,1,3,0:T(8,128)S(1)} %get-tuple-element.330, f32[4,8,256]{2,1,0:T(8,128)S(1)} %max.25, pred[256,256]{0,1:T(8,128)(4,1)S(1)} %and_and_fusion.3), kind=kLoop, calls=%fused_computation.5.clone.1 | loop fusion | flops 10477568 | bytes 8519680 | tf_op jit(solution)/shard_map/while/body/eval_jaxpr/reduce_sum | solution.py:56
  42.3 3.7 %multiply_add_fusion.5 = f32[4,8,256,128]{3,2,1,0:T(8,128)S(1)} fusion(f32[4,8,256,128]{3,2,1,0:T(8,128)S(1)} %copy-done, f32[4,8,256]{2,1,0:T(8,128)S(1)} %get-tuple-element.332, bf16[256,4,128,1]{0,2,3,1:T(8,128)(2,1)S(1)} %bitcast.76, f32[4,256,256,8]{2,1,3,0:T(8,128)S(1)} %get-tuple-element.330, f32[4,8,256]{2,1,0:T(8,128)S(1)} %max.25, ...), kind=kOutput, calls=%fused_computation.7.clone.1 | convolution fusion | flops 549453824 | bytes 17170432 | tf_op jit(solution)/shard_map/while/body/eval_jaxpr/kgtp,pkd->kgtd/dot_general | solution.py:57
  46.1 1.9 %copy-done.1 = f32[4,8,256,128]{3,2,1,0:T(8,128)} copy-done((f32[4,8,256,128]{3,2,1,0:T(8,128)}, f32[4,8,256,128]{3,2,1,0:T(8,128)S(1)}, u32[]{:S(2)}) %copy-start.1) | copy-done | bytes 4194328 | tf_op jit(solution)/shard_map/while
  48.0 2.2 %collective-permute-start = (bf16[2,256,512]{1,2,0:T(8,128)(2,1)S(1)}, bf16[2,256,512]{1,2,0:T(8,128)(2,1)S(1)}, u32[]{:S(2)}, u32[]{:S(2)}) collective-permute-start(bf16[2,256,512]{1,2,0:T(8,128)(2,1)S(1)} %get-tuple-element.350), channel_id=1, source_target_pairs={{0,2},{2,4},{4,6},{6,8},{8,10},{10,12},{12,14},{1,3},{3,5},{5,7},{... | collective-permute-start | bytes 1572872 | tf_op jit(solution)/shard_map/while/body/eval_jaxpr/ppermute | solution.py:21
  51.2 11.4 %collective-permute-done = bf16[2,256,512]{1,2,0:T(8,128)(2,1)S(1)} collective-permute-done((bf16[2,256,512]{1,2,0:T(8,128)(2,1)S(1)}, bf16[2,256,512]{1,2,0:T(8,128)(2,1)S(1)}, u32[]{:S(2)}, u32[]{:S(2)}) %collective-permute-start) | collective-permute-done | bytes 524320 | tf_op jit(solution)/shard_map/while/body/eval_jaxpr/ppermute | solution.py:21
  62.7 1.5 %fusion.61 = (f32[4,8,256]{2,1,0:T(8,128)S(1)}, f32[4,256,256,8]{2,1,3,0:T(8,128)S(1)}) fusion(pred[256,256]{0,1:T(8,128)(4,1)S(1)} %and_and_fusion.3, bf16[256,4,128,1]{0,2,3,1:T(8,128)(2,1)S(1)} %bitcast.70, bf16[256,4,8,128]{3,0,2,1:T(8,128)(2,1)S(1)} %get-tuple-element.366), kind=kOutput, calls=%fused_computation.3.clone.1 | convolution fusion | flops 543154176 | bytes 10846208 | tf_op jit(solution)/shard_map/while/body/eval_jaxpr/tkgd,pkd->kgtp/dot_general | solution.py:44
  64.2 2.1 %fusion.62 = f32[4,8,256]{2,1,0:T(8,128)S(1)} fusion(f32[4,256,256,8]{2,1,3,0:T(8,128)S(1)} %get-tuple-element.330, f32[4,8,256]{2,1,0:T(8,128)S(1)} %max.25, pred[256,256]{0,1:T(8,128)(4,1)S(1)} %and_and_fusion.3), kind=kLoop, calls=%fused_computation.5.clone.1 | loop fusion | flops 10477568 | bytes 8519680 | tf_op jit(solution)/shard_map/while/body/eval_jaxpr/reduce_sum | solution.py:56
  66.4 3.7 %multiply_add_fusion.5 = f32[4,8,256,128]{3,2,1,0:T(8,128)S(1)} fusion(f32[4,8,256,128]{3,2,1,0:T(8,128)S(1)} %copy-done, f32[4,8,256]{2,1,0:T(8,128)S(1)} %get-tuple-element.332, bf16[256,4,128,1]{0,2,3,1:T(8,128)(2,1)S(1)} %bitcast.76, f32[4,256,256,8]{2,1,3,0:T(8,128)S(1)} %get-tuple-element.330, f32[4,8,256]{2,1,0:T(8,128)S(1)} %max.25, ...), kind=kOutput, calls=%fused_computation.7.clone.1 | convolution fusion | flops 549453824 | bytes 17170432 | tf_op jit(solution)/shard_map/while/body/eval_jaxpr/kgtp,pkd->kgtd/dot_general | solution.py:57
  70.2 1.9 %copy-done.1 = f32[4,8,256,128]{3,2,1,0:T(8,128)} copy-done((f32[4,8,256,128]{3,2,1,0:T(8,128)}, f32[4,8,256,128]{3,2,1,0:T(8,128)S(1)}, u32[]{:S(2)}) %copy-start.1) | copy-done | bytes 4194328 | tf_op jit(solution)/shard_map/while
  72.1 1.9 %collective-permute-start = (bf16[2,256,512]{1,2,0:T(8,128)(2,1)S(1)}, bf16[2,256,512]{1,2,0:T(8,128)(2,1)S(1)}, u32[]{:S(2)}, u32[]{:S(2)}) collective-permute-start(bf16[2,256,512]{1,2,0:T(8,128)(2,1)S(1)} %get-tuple-element.350), channel_id=1, source_target_pairs={{0,2},{2,4},{4,6},{6,8},{8,10},{10,12},{12,14},{1,3},{3,5},{5,7},{... | collective-permute-start | bytes 1572872 | tf_op jit(solution)/shard_map/while/body/eval_jaxpr/ppermute | solution.py:21
  75.0 10.8 %collective-permute-done = bf16[2,256,512]{1,2,0:T(8,128)(2,1)S(1)} collective-permute-done((bf16[2,256,512]{1,2,0:T(8,128)(2,1)S(1)}, bf16[2,256,512]{1,2,0:T(8,128)(2,1)S(1)}, u32[]{:S(2)}, u32[]{:S(2)}) %collective-permute-start) | collective-permute-done | bytes 524320 | tf_op jit(solution)/shard_map/while/body/eval_jaxpr/ppermute | solution.py:21
  87.4 2.1 %fusion.62 = f32[4,8,256]{2,1,0:T(8,128)S(1)} fusion(f32[4,256,256,8]{2,1,3,0:T(8,128)S(1)} %get-tuple-element.330, f32[4,8,256]{2,1,0:T(8,128)S(1)} %max.25, pred[256,256]{0,1:T(8,128)(4,1)S(1)} %and_and_fusion.3), kind=kLoop, calls=%fused_computation.5.clone.1 | loop fusion | flops 10477568 | bytes 8519680 | tf_op jit(solution)/shard_map/while/body/eval_jaxpr/reduce_sum | solution.py:56
  89.6 3.7 %multiply_add_fusion.5 = f32[4,8,256,128]{3,2,1,0:T(8,128)S(1)} fusion(f32[4,8,256,128]{3,2,1,0:T(8,128)S(1)} %copy-done, f32[4,8,256]{2,1,0:T(8,128)S(1)} %get-tuple-element.332, bf16[256,4,128,1]{0,2,3,1:T(8,128)(2,1)S(1)} %bitcast.76, f32[4,256,256,8]{2,1,3,0:T(8,128)S(1)} %get-tuple-element.330, f32[4,8,256]{2,1,0:T(8,128)S(1)} %max.25, ...), kind=kOutput, calls=%fused_computation.7.clone.1 | convolution fusion | flops 549453824 | bytes 17170432 | tf_op jit(solution)/shard_map/while/body/eval_jaxpr/kgtp,pkd->kgtd/dot_general | solution.py:57
  93.4 1.9 %copy-done.1 = f32[4,8,256,128]{3,2,1,0:T(8,128)} copy-done((f32[4,8,256,128]{3,2,1,0:T(8,128)}, f32[4,8,256,128]{3,2,1,0:T(8,128)S(1)}, u32[]{:S(2)}) %copy-start.1) | copy-done | bytes 4194328 | tf_op jit(solution)/shard_map/while
  95.3 1.9 %collective-permute-start = (bf16[2,256,512]{1,2,0:T(8,128)(2,1)S(1)}, bf16[2,256,512]{1,2,0:T(8,128)(2,1)S(1)}, u32[]{:S(2)}, u32[]{:S(2)}) collective-permute-start(bf16[2,256,512]{1,2,0:T(8,128)(2,1)S(1)} %get-tuple-element.350), channel_id=1, source_target_pairs={{0,2},{2,4},{4,6},{6,8},{8,10},{10,12},{12,14},{1,3},{3,5},{5,7},{... | collective-permute-start | bytes 1572872 | tf_op jit(solution)/shard_map/while/body/eval_jaxpr/ppermute | solution.py:21
  98.2 9.9 %collective-permute-done = bf16[2,256,512]{1,2,0:T(8,128)(2,1)S(1)} collective-permute-done((bf16[2,256,512]{1,2,0:T(8,128)(2,1)S(1)}, bf16[2,256,512]{1,2,0:T(8,128)(2,1)S(1)}, u32[]{:S(2)}, u32[]{:S(2)}) %collective-permute-start) | collective-permute-done | bytes 524320 | tf_op jit(solution)/shard_map/while/body/eval_jaxpr/ppermute | solution.py:21
  109.7 2.1 %fusion.62 = f32[4,8,256]{2,1,0:T(8,128)S(1)} fusion(f32[4,256,256,8]{2,1,3,0:T(8,128)S(1)} %get-tuple-element.330, f32[4,8,256]{2,1,0:T(8,128)S(1)} %max.25, pred[256,256]{0,1:T(8,128)(4,1)S(1)} %and_and_fusion.3), kind=kLoop, calls=%fused_computation.5.clone.1 | loop fusion | flops 10477568 | bytes 8519680 | tf_op jit(solution)/shard_map/while/body/eval_jaxpr/reduce_sum | solution.py:56
  111.9 3.7 %multiply_add_fusion.5 = f32[4,8,256,128]{3,2,1,0:T(8,128)S(1)} fusion(f32[4,8,256,128]{3,2,1,0:T(8,128)S(1)} %copy-done, f32[4,8,256]{2,1,0:T(8,128)S(1)} %get-tuple-element.332, bf16[256,4,128,1]{0,2,3,1:T(8,128)(2,1)S(1)} %bitcast.76, f32[4,256,256,8]{2,1,3,0:T(8,128)S(1)} %get-tuple-element.330, f32[4,8,256]{2,1,0:T(8,128)S(1)} %max.25, ...), kind=kOutput, calls=%fused_computation.7.clone.1 | convolution fusion | flops 549453824 | bytes 17170432 | tf_op jit(solution)/shard_map/while/body/eval_jaxpr/kgtp,pkd->kgtd/dot_general | solution.py:57
  115.7 1.9 %copy-done.1 = f32[4,8,256,128]{3,2,1,0:T(8,128)} copy-done((f32[4,8,256,128]{3,2,1,0:T(8,128)}, f32[4,8,256,128]{3,2,1,0:T(8,128)S(1)}, u32[]{:S(2)}) %copy-start.1) | copy-done | bytes 4194328 | tf_op jit(solution)/shard_map/while
  117.5 3.1 %fusion.33 = bf16[256,4,8,128]{3,0,2,1:T(8,128)(2,1)S(1)} fusion(f32[4,8,256,128]{3,2,1,0:T(8,128)} %get-tuple-element.172, f32[4,8,256]{2,1,0:T(8,128)S(1)} %get-tuple-element.173), kind=kLoop, calls=%fused_computation.44 | loop fusion | flops 2097152 | bytes 6324224 | tf_op jit(solution)/shard_map/convert_element_type | solution.py:89
  123.4 6.4 %psum.21 = f32[256]{0:T(256)S(1)} all-reduce(f32[256]{0:T(256)S(1)} %fusion.20), channel_id=1, replica_groups=mesh['branch'=2,'ctx'=8,'tp'=2] {'tp'}, use_global_device_ids=true, to_apply=%region_7.8 | all-reduce | flops 256 | bytes 2048 | tf_op jit(solution)/shard_map/psum | solution.py:93
  129.9 2.2 %fusion.24 = (f32[256]{0:T(256)S(1)}, bf16[1,256,4096]{2,1,0:T(8,128)(2,1)}) fusion(bf16[256,4096]{1,0:T(8,128)(2,1)S(1)} %bitcast.72, f32[4096]{0:T(1024)S(1)} %bitcast.79, f32[4096]{0:T(1024)S(1)} %bitcast.80, f32[256]{0:T(256)S(1)} %add_rsqrt_fusion), kind=kLoop, calls=%fused_computation.33 | loop fusion | flops 6291200 | bytes 4229120 | tf_op jit(solution)/shard_map/reduce_sum | solution.py:95
  132.1 2.5 %psum.22 = f32[256]{0:T(256)S(1)} all-reduce(f32[256]{0:T(256)S(1)} %get-tuple-element.254), channel_id=1, replica_groups=mesh['branch'=2,'ctx'=8,'tp'=2] {'tp'}, use_global_device_ids=true, to_apply=%region_9.10 | all-reduce | flops 256 | bytes 2048 | tf_op jit(solution)/shard_map/psum | solution.py:96
  134.5 4.3 %psum.23 = f32[256]{0:T(256)} all-reduce(f32[256]{0:T(256)S(1)} %psum.22), channel_id=1, replica_groups=mesh['branch'=2,'ctx'=8,'tp'=2] {'branch'}, use_global_device_ids=true, to_apply=%region_10.11 | all-reduce | flops 256 | bytes 2048 | tf_op jit(solution)/shard_map/psum | solution.py:98
  (69 shorter events, 16.9 us)
Async XLA Ops:
  23.0 15.6 %collective-permute-start = (bf16[2,256,512]{1,2,0:T(8,128)(2,1)S(1)}, bf16[2,256,512]{1,2,0:T(8,128)(2,1)S(1)}, u32[]{:S(2)}, u32[]{:S(2)}) collective-permute-start(bf16[2,256,512]{1,2,0:T(8,128)(2,1)S(1)} %get-tuple-element.350), channel_id=1, source_target_pairs={{0,2},{2,4},{4,6},{6,8},{8,10},{10,12},{12,14},{1,3},{3,5},{5,7},{... | collective-permute-start | bytes 1572872 | tf_op jit(solution)/shard_map/while/body/eval_jaxpr/ppermute | solution.py:21
  38.6 3.7 %copy-start = (f32[4,8,256,128]{3,2,1,0:T(8,128)S(1)}, f32[4,8,256,128]{3,2,1,0:T(8,128)}, u32[]{:S(2)}) copy-start(f32[4,8,256,128]{3,2,1,0:T(8,128)} %get-tuple-element.349) | copy-start | bytes 12582916 | tf_op jit(solution)/shard_map/while
  46.1 1.9 %copy-start.1 = (f32[4,8,256,128]{3,2,1,0:T(8,128)}, f32[4,8,256,128]{3,2,1,0:T(8,128)S(1)}, u32[]{:S(2)}) copy-start(f32[4,8,256,128]{3,2,1,0:T(8,128)S(1)} %multiply_add_fusion.5) | copy-start | bytes 12582916 | tf_op jit(solution)/shard_map/while
  48.0 14.6 %collective-permute-start = (bf16[2,256,512]{1,2,0:T(8,128)(2,1)S(1)}, bf16[2,256,512]{1,2,0:T(8,128)(2,1)S(1)}, u32[]{:S(2)}, u32[]{:S(2)}) collective-permute-start(bf16[2,256,512]{1,2,0:T(8,128)(2,1)S(1)} %get-tuple-element.350), channel_id=1, source_target_pairs={{0,2},{2,4},{4,6},{6,8},{8,10},{10,12},{12,14},{1,3},{3,5},{5,7},{... | collective-permute-start | bytes 1572872 | tf_op jit(solution)/shard_map/while/body/eval_jaxpr/ppermute | solution.py:21
  62.7 3.7 %copy-start = (f32[4,8,256,128]{3,2,1,0:T(8,128)S(1)}, f32[4,8,256,128]{3,2,1,0:T(8,128)}, u32[]{:S(2)}) copy-start(f32[4,8,256,128]{3,2,1,0:T(8,128)} %get-tuple-element.349) | copy-start | bytes 12582916 | tf_op jit(solution)/shard_map/while
  70.2 1.9 %copy-start.1 = (f32[4,8,256,128]{3,2,1,0:T(8,128)}, f32[4,8,256,128]{3,2,1,0:T(8,128)S(1)}, u32[]{:S(2)}) copy-start(f32[4,8,256,128]{3,2,1,0:T(8,128)S(1)} %multiply_add_fusion.5) | copy-start | bytes 12582916 | tf_op jit(solution)/shard_map/while
  72.1 13.7 %collective-permute-start = (bf16[2,256,512]{1,2,0:T(8,128)(2,1)S(1)}, bf16[2,256,512]{1,2,0:T(8,128)(2,1)S(1)}, u32[]{:S(2)}, u32[]{:S(2)}) collective-permute-start(bf16[2,256,512]{1,2,0:T(8,128)(2,1)S(1)} %get-tuple-element.350), channel_id=1, source_target_pairs={{0,2},{2,4},{4,6},{6,8},{8,10},{10,12},{12,14},{1,3},{3,5},{5,7},{... | collective-permute-start | bytes 1572872 | tf_op jit(solution)/shard_map/while/body/eval_jaxpr/ppermute | solution.py:21
  85.9 3.7 %copy-start = (f32[4,8,256,128]{3,2,1,0:T(8,128)S(1)}, f32[4,8,256,128]{3,2,1,0:T(8,128)}, u32[]{:S(2)}) copy-start(f32[4,8,256,128]{3,2,1,0:T(8,128)} %get-tuple-element.349) | copy-start | bytes 12582916 | tf_op jit(solution)/shard_map/while
  93.4 1.9 %copy-start.1 = (f32[4,8,256,128]{3,2,1,0:T(8,128)}, f32[4,8,256,128]{3,2,1,0:T(8,128)S(1)}, u32[]{:S(2)}) copy-start(f32[4,8,256,128]{3,2,1,0:T(8,128)S(1)} %multiply_add_fusion.5) | copy-start | bytes 12582916 | tf_op jit(solution)/shard_map/while
  95.3 12.8 %collective-permute-start = (bf16[2,256,512]{1,2,0:T(8,128)(2,1)S(1)}, bf16[2,256,512]{1,2,0:T(8,128)(2,1)S(1)}, u32[]{:S(2)}, u32[]{:S(2)}) collective-permute-start(bf16[2,256,512]{1,2,0:T(8,128)(2,1)S(1)} %get-tuple-element.350), channel_id=1, source_target_pairs={{0,2},{2,4},{4,6},{6,8},{8,10},{10,12},{12,14},{1,3},{3,5},{5,7},{... | collective-permute-start | bytes 1572872 | tf_op jit(solution)/shard_map/while/body/eval_jaxpr/ppermute | solution.py:21
  108.1 3.7 %copy-start = (f32[4,8,256,128]{3,2,1,0:T(8,128)S(1)}, f32[4,8,256,128]{3,2,1,0:T(8,128)}, u32[]{:S(2)}) copy-start(f32[4,8,256,128]{3,2,1,0:T(8,128)} %get-tuple-element.349) | copy-start | bytes 12582916 | tf_op jit(solution)/shard_map/while
  115.6 1.9 %copy-start.1 = (f32[4,8,256,128]{3,2,1,0:T(8,128)}, f32[4,8,256,128]{3,2,1,0:T(8,128)S(1)}, u32[]{:S(2)}) copy-start(f32[4,8,256,128]{3,2,1,0:T(8,128)S(1)} %multiply_add_fusion.5) | copy-start | bytes 12582916 | tf_op jit(solution)/shard_map/while
  117.5 12.4 %copy-start.2 = (f32[1,4096]{1,0:T(1,128)S(1)}, f32[1,4096]{1,0:T(1,128)}, u32[]{:S(2)}) copy-start(f32[1,4096]{1,0:T(1,128)} %param.13) | copy-start | bytes 49156
  117.5 12.4 %copy-start.3 = (f32[1,4096]{1,0:T(1,128)S(1)}, f32[1,4096]{1,0:T(1,128)}, u32[]{:S(2)}) copy-start(f32[1,4096]{1,0:T(1,128)} %param.12) | copy-start | bytes 49156
where the time goes:
time: 140 us; the launch traced here: 139 us
  waiting for transfers between devices  43.7 us (31%)
  matrix products  28.8 us (21%)
  local copies, waits for them, and re-layouts  24.6 us (18%)
  other arithmetic  18.3 us (13%)
  blocking collectives  13.2 us (9%)
  starting transfers between devices  9.17 us (7%)
    ppermute x4, waiting for transfers between devices, shifted(): return lax.ppermute(block, axis, route)  43.7 us
    dot_general x5, matrix products, absorb(): jnp.einsum('kgtp,pkd->kgtd', weights.astype(jnp.bfloat16), value_rows, pr...  19.7 us
    reduce_sum x5, other arithmetic, absorb(): totals = totals * rescale + jnp.sum(weights, axis=-1)  10.6 us
    unnamed x9, local copies, waits for them, and re-layouts  10.3 us
    ppermute x4, starting transfers between devices, shifted(): return lax.ppermute(block, axis, route)  9.17 us
    dot_general x5, matrix products, absorb(): jnp.einsum('tkgd,pkd->kgtp', query_rows, key_rows, preferred_element_type...  9.09 us
    while x24, local copies, waits for them, and re-layouts  7.67 us
    psum x1, blocking collectives, local(): square_sum = lax.psum(squares, 'tp')  6.43 us
  transfers between devices with their start and end apart: 4, of which 4 were waited for; matrix products, arithmetic and copies ran while one was open for 3% of the time, Pallas kernels for 0%

commit v1 on v0

v1 whole, which is shorter than its diff:
```python
import functools
import math

import jax
import jax.numpy as jnp
from jax import lax
from jax.experimental import pallas as pl
from jax.experimental.pallas import tpu as pltpu
from jax.sharding import PartitionSpec as P

H = 64
KVH = 8
HD = 128
D = 8192

BIG = 2.0**100
EPSILON = 1e-06
MESH = pl.DeviceIdType.MESH


def kernel(
    sizes, q_hbm, k_hbm, v_hbm, seg_ref, gain_ref, weight_ref,
    att_ref, inv_ref, joined_ref,
    q_vm, kv, gmask, fmask, acc, best, squares, scored, stats,
    q_sem, own_sem, col_send, col_recv, x_send, x_recv, st_send, st_recv,
):
    n, branches, tps, span = sizes
    steps = span // 2
    rows = q_vm.shape[0]
    half = rows // 2
    groups = kv.shape[0]
    per_group = H // KVH
    window = kv.shape[2]
    scale = math.log2(math.e) / math.sqrt(HD)
    me = lax.axis_index("ctx")
    b_me, t_me = lax.axis_index("branch"), lax.axis_index("tp")
    side = lax.rem(me, 2)
    partner = me + 1 - 2 * side
    has_next = me + 2 < n
    mine = b_me * tps + t_me

    q_copy = pltpu.make_async_copy(q_hbm.at[0], q_vm, q_sem)
    own = []
    for g in range(groups):
        for part, source in enumerate((k_hbm, v_hbm)):
            own.append(
                pltpu.make_async_copy(
                    source.at[0, :, pl.ds(g * HD, HD)],
                    kv.at[g, part, pl.ds(span * rows, rows), :],
                    own_sem.at[g, part],
                )
            )
    for copy in own:
        copy.start()
    q_copy.start()

    peers = []
    for db in range(branches):
        for dt in range(tps):
            if db or dt:
                peers.append((lax.rem(b_me + db, branches), lax.rem(t_me + dt, tps)))

    barrier = pltpu.get_barrier_semaphore()

    @pl.when(me >= 2)
    def _():
        pl.semaphore_signal(barrier, inc=1, device_id={"ctx": me - 2}, device_id_type=MESH)

    @pl.when(has_next)
    def _():
        pl.semaphore_signal(barrier, inc=1, device_id={"ctx": me + 2}, device_id_type=MESH)

    pl.semaphore_signal(barrier, inc=1, device_id={"ctx": partner}, device_id_type=MESH)
    for b_to, t_to in peers:
        pl.semaphore_signal(
            barrier, inc=1, device_id={"branch": b_to, "tp": t_to}, device_id_type=MESH
        )

    lane = lax.broadcasted_iota(jnp.int32, (1, HD), 1)
    segs = seg_ref[...]
    total = segs.shape[0] * segs.shape[1]
    far = 2.0**30
    low = jnp.where(lane == 0, 0.0, jnp.where(lane == 4, -far, far))
    high = jnp.where(lane == 3, float(total), jnp.where(lane == 4, 0.0, -far))
    for rollout in range(1, 4):
        count = jnp.sum((segs < rollout).astype(jnp.float32), axis=1, keepdims=True)
        count = jnp.sum(count, axis=0, keepdims=True)
        low = jnp.where(lane == rollout, count, low)
        high = jnp.where(lane == rollout - 1, count, high)
    place = lax.broadcasted_iota(jnp.int32, (window, HD), 0) + (me - span) * rows
    place = place.astype(jnp.float32)
    member = jnp.where((place >= low) & (place < high), 1.0, 0.0)
    gmask[...] = member.astype(jnp.bfloat16)
    fmask[...] = ((member[span * rows :] - 1.0) * BIG).astype(jnp.bfloat16)
    squares[...] = jnp.zeros_like(squares)
    scored[...] = jnp.zeros_like(scored)

    for distance in range(1, span + 1):

        @pl.when(me < distance)
        def _(distance=distance):
            kv[:, :, pl.ds((span - distance) * rows, rows), :] = jnp.zeros(
                (groups, 2, rows, HD), jnp.bfloat16
            )

    def col_copy(step, g):
        return pltpu.make_async_remote_copy(
            src_ref=kv.at[g, :, pl.ds((span - 2 * (step - 1)) * rows, rows), :],
            dst_ref=kv.at[g, :, pl.ds((span - 2 * step) * rows, rows), :],
            send_sem=col_send.at[step - 1, g],
            recv_sem=col_recv.at[step - 1, g],
            device_id={"ctx": me + 2},
            device_id_type=MESH,
        )

    def x_copy(u, g):
        first = pl.multiple_of((span - 2 * u - 2 * side) * rows, rows)
        return pltpu.make_async_remote_copy(
            src_ref=kv.at[g, :, pl.ds(first, rows), :],
            dst_ref=kv.at[g, :, pl.ds((span - 2 * u - 1) * rows, rows), :],
            send_sem=x_send.at[u, g],
            recv_sem=x_recv.at[u, g],
            device_id={"ctx": partner},
            device_id_type=MESH,
        )

    pl.semaphore_wait(
        barrier,
        1 + len(peers) + (me >= 2).astype(jnp.int32) + has_next.astype(jnp.int32),
    )

    for g in range(groups):
        own[2 * g].wait()
        own[2 * g + 1].wait()

        @pl.when(has_next)
        def _(g=g):
            col_copy(1, g).start()

        @pl.when(side == 0)
        def _(g=g):
            x_copy(0, g).start()

    def arrive(step, g):
        @pl.when(me >= 2 * step)
        def _():
            col_copy(step, g).wait_recv()
            if step < steps:

                @pl.when(has_next)
                def _():
                    col_copy(step + 1, g).start()

                @pl.when(side == 0)
                def _():
                    x_copy(step, g).start()

            @pl.when(side == 1)
            def _():
                x_copy(step - 1, g).start()

    tri_row = lax.broadcasted_iota(jnp.int32, (2 * half, half), 0)
    tri_col = lax.broadcasted_iota(jnp.int32, (2 * half, half), 1)
    causal = tri_col <= lax.rem(tri_row, half)

    def pair(step, g, index):
        top = g * per_group + 2 * index
        for r in range(2):
            lines = pl.ds(r * half, half)
            first, last = (span - 2 * step) * rows, (span - 2 * step + 2) * rows
            if step == 1:
                last = span * rows + (r + 1) * half
            if step == steps:
                first += r * half
            keys = pl.ds(first, last - first)
            columns = [pl.ds(pl.multiple_of((top + e) * HD, HD), HD) for e in range(2)]
            marks = fmask[lines, :]
            left = jnp.concatenate(
                [
                    jnp.concatenate([q_vm[lines, columns[0]], q_vm[lines, columns[1]]], axis=0),
                    jnp.concatenate([marks, marks], axis=0),
                ],
                axis=1,
            )
            right = jnp.concatenate([kv[g, 0, keys, :], gmask[keys, :]], axis=1)
            scores = lax.dot_general(
                left, right, (((1,), (1,)), ((), ())), preferred_element_type=jnp.float32
            )
            if step == 1:
                body = last - first - half
                scores = jnp.concatenate(
                    [scores[:, :body], jnp.where(causal, scores[:, body:], -BIG)], axis=1
                )
            peak = jnp.max(scores, axis=1, keepdims=True)
            if step > 1:
                before = best[top, lines, :], best[top + 1, lines, :]
                before = jnp.concatenate(before, axis=0)
                wide = jnp.maximum(before, peak)
                peak = wide[:, :1]
            weights = jnp.exp2((scores - peak) * scale).astype(jnp.bfloat16)
            mixer = jnp.concatenate(
                [kv[g, 1, keys, :], jnp.ones((last - first, HD), jnp.bfloat16)], axis=1
            )
            mixed = jnp.dot(weights, mixer, preferred_element_type=jnp.float32)
            if step > 1:
                shrink = jnp.exp2((before - wide) * scale)
                earlier = jnp.concatenate(
                    [acc[top, lines, :], acc[top + 1, lines, :]], axis=0
                )
                mixed = mixed + earlier * jnp.concatenate([shrink, shrink], axis=1)
            if step < steps:
                acc[top, lines, :] = mixed[:half]
                acc[top + 1, lines, :] = mixed[half:]
                wide = jnp.broadcast_to(peak, (2 * half, HD))
                best[top, lines, :] = wide[:half]
                best[top + 1, lines, :] = wide[half:]
            else:
                attended = (mixed[:, :HD] / mixed[:, HD:]).astype(jnp.bfloat16)
                for e in range(2):
                    out = attended[e * half : (e + 1) * half]
                    att_ref[lines, columns[e]] = out
                    out = out.astype(jnp.float32)
                    line = gain_ref[:, columns[e]] * weight_ref[:, columns[e]]
                    squares[lines, :] += out * out
                    scored[lines, :] += out * line

    units = [(step, g) for step in range(1, steps + 1) for g in range(groups)]
    pairs = per_group // 2
    arrive(*units[0])
    q_copy.wait()
    for number, (step, g) in enumerate(units):

        @pl.when(me >= 2 * step - 1)
        def _(step=step, g=g):
            x_copy(step - 1, g).wait_recv()

        def walk(index, carry, step=step, g=g):
            pair(step, g, index)
            return carry

        lax.fori_loop(0, pairs // 2, walk, 0)
        if number + 1 < len(units):
            arrive(*units[number + 1])
        lax.fori_loop(pairs // 2, pairs, walk, 0)

    slab = jnp.concatenate(
        [
            jnp.sum(squares[...].T, axis=0, keepdims=True),
            jnp.sum(scored[...].T, axis=0, keepdims=True),
            jnp.zeros((6, rows), jnp.float32),
        ],
        axis=0,
    )
    stats[mine] = slab

    def stat_copy(number):
        b_to, t_to = peers[number]
        return pltpu.make_async_remote_copy(
            src_ref=stats.at[mine],
            dst_ref=stats.at[mine],
            send_sem=st_send.at[number],
            recv_sem=st_recv.at[number],
            device_id={"branch": b_to, "tp": t_to},
            device_id_type=MESH,
        )

    for number in range(len(peers)):
        stat_copy(number).start()

    for g in range(groups):
        for step in range(1, steps + 1):

            @pl.when(has_next & (me >= 2 * (step - 1)))
            def _(step=step, g=g):
                col_copy(step, g).wait_send()

            @pl.when(me >= 2 * (step - 1 + side))
            def _(step=step, g=g):
                x_copy(step - 1, g).wait_send()

    for number in range(len(peers)):
        stat_copy(number).wait()

    def inverse_of(branch):
        square_sum = stats[branch * tps, 0:1, :]
        score = stats[branch * tps, 1:2, :]
        for t in range(1, tps):
            square_sum = square_sum + stats[branch * tps + t, 0:1, :]
            score = score + stats[branch * tps + t, 1:2, :]
        return lax.rsqrt(square_sum / D + EPSILON), score

    joined = jnp.zeros((1, rows), jnp.float32)
    for branch in range(branches):
        inverse, score = inverse_of(branch)
        joined = joined + inverse * score
    joined_ref[...] = joined
    inverse, _ = inverse_of(b_me)
    inv_ref[...] = jnp.broadcast_to(inverse, (HD, rows)).T


def local(sizes, queries, keys, values, segments, norm_gain, head_weight):
    n, branches, tps, span = sizes
    rows, columns = queries.shape[1:]
    groups = keys.shape[2] // HD
    heads = columns // HD
    window = (span + 1) * rows
    steps = span // 2
    devices = branches * tps
    vmem = pl.BlockSpec(memory_space=pltpu.VMEM)
    hbm = pl.BlockSpec(memory_space=pl.ANY)
    dma = pltpu.SemaphoreType.DMA
    attended, inverse, joined = pl.pallas_call(
        functools.partial(kernel, sizes),
        out_shape=(
            jax.ShapeDtypeStruct((rows, columns), jnp.bfloat16),
            jax.ShapeDtypeStruct((rows, HD), jnp.float32),
            jax.ShapeDtypeStruct((1, rows), jnp.float32),
        ),
        in_specs=[hbm, hbm, hbm, vmem, vmem, vmem],
        out_specs=(vmem, vmem, vmem),
        scratch_shapes=[
            pltpu.VMEM((rows, columns), jnp.bfloat16),
            pltpu.VMEM((groups, 2, window, HD), jnp.bfloat16),
            pltpu.VMEM((window, HD), jnp.bfloat16),
            pltpu.VMEM((rows, HD), jnp.bfloat16),
            pltpu.VMEM((heads, rows, 2 * HD), jnp.float32),
            pltpu.VMEM((heads, rows, HD), jnp.float32),
            pltpu.VMEM((rows, HD), jnp.float32),
            pltpu.VMEM((rows, HD), jnp.float32),
            pltpu.VMEM((devices, 8, rows), jnp.float32),
            dma,
            dma((groups, 2)),
            dma((steps, groups)),
            dma((steps, groups)),
            dma((steps, groups)),
            dma((steps, groups)),
            dma((devices - 1,)),
            dma((devices - 1,)),
        ],
        compiler_params=pltpu.CompilerParams(
            collective_id=0, has_side_effects=True, vmem_limit_bytes=48 * 2**20
        ),
        cost_estimate=pl.CostEstimate(
            flops=4 * rows * window * columns,
            bytes_accessed=4 * rows * columns,
            transcendentals=heads * rows * window,
        ),
    )(queries, keys, values, segments.reshape(-1, HD), norm_gain, head_weight)
    normed = attended.astype(jnp.float32) * inverse[:, :1] * norm_gain
    return normed.astype(jnp.bfloat16)[None], joined.reshape(rows)


def solution(mesh):
    n = mesh.shape["ctx"]
    sizes = (n, mesh.shape["branch"], mesh.shape["tp"], n // 2)
    return jax.shard_map(
        functools.partial(local, sizes),
        mesh=mesh,
        in_specs=(
            P("branch", "ctx", "tp"),
            P("branch", "ctx", "tp"),
            P("branch", "ctx", "tp"),
            P(),
            P("branch", "tp"),
            P("branch", "tp"),
        ),
        out_specs=(P("branch", "ctx", "tp"), P("ctx")),
        check_vma=False,
    )
```

time: 140 us -> 57 us (0.41)
  Pallas kernels: 0 us -> 47.7 us
  waiting for transfers between devices: 43.7 us -> 0 us
  matrix products: 28.8 us -> 0 us
  local copies, waits for them, and re-layouts: 24.6 us -> 6.28 us
  other arithmetic: 18.3 us -> 1.97 us
  blocking collectives: 13.2 us -> 0 us
  starting transfers between devices: 9.17 us -> 0 us
    pallas_call x0 -> x1, Pallas kernels: none -> 47.7 us  [local(): pl.pallas_call(functools.partial(kernel, sizes), out_shape=(jax.ShapeDtyp...]
    ppermute x4 -> x0, waiting for transfers between devices: 43.7 us -> none  [shifted(): return lax.ppermute(block, axis, route)]
    dot_general x10 -> x0, matrix products: 28.8 us -> none  [the longest x5 19.7 us: absorb(): jnp.einsum('kgtp,pkd->kgtd', weights.astype(jnp.bfloat16), value_rows, pr...]
    reduce_sum x7 -> x0, other arithmetic: 13.3 us -> none  [the longest x5 10.6 us: absorb(): totals = totals * rescale + jnp.sum(weights, axis=-1)]
    psum x3 -> x0, blocking collectives: 13.2 us -> none  [the longest x1 6.43 us: local(): square_sum = lax.psum(squares, 'tp')]
    ppermute x4 -> x0, starting transfers between devices: 9.17 us -> none  [shifted(): return lax.ppermute(block, axis, route)]
    while x24 -> x0, local copies, waits for them, and re-layouts: 7.67 us -> none
    unnamed x9 -> x13, local copies, waits for them, and re-layouts: 10.3 us -> 6.18 us
  transfers between devices with their start and end apart: 4 -> 0, of which waited for: 4 -> 0; matrix products, arithmetic and copies ran while one was open for 3% -> 0% of each run, Pallas kernels for 0% -> 0%
where the time goes in v1:
time: 57 us; the launch traced here: 56.6 us
  Pallas kernels  47.7 us (84%)
  local copies, waits for them, and re-layouts  6.28 us (11%)
  other arithmetic  1.97 us (3%)
  between operations  0.66 us (1%)
    pallas_call x1, Pallas kernels, local(): pl.pallas_call(functools.partial(kernel, sizes), out_shape=(jax.ShapeDtyp...  47.7 us
    unnamed x13, local copies, waits for them, and re-layouts  6.18 us
    broadcast_in_dim x1, other arithmetic, local(): return (normed.astype(jnp.bfloat16)[None], joined.reshape(rows))  1.97 us

profile of v1, /device:TPU:25, one launch (start us, length us, event | category | flops | bytes accessed | tf_op | source)
XLA Modules:
  0.0 56.6 jit_solution(12055422545839583369)
XLA Ops:
  0.6 0.0 copy-start
  0.6 0.7 %copy-done = f32[1,4096]{1,0:T(1,128)S(1)} copy-done((f32[1,4096]{1,0:T(1,128)S(1)}, f32[1,4096]{1,0:T(1,128)}, u32[]{:S(2)}) %copy-start) | copy-done | bytes 16408
  1.4 0.0 copy-start.1
  1.4 1.6 %copy-done.1 = bf16[1,256,4096]{2,1,0:T(8,128)(2,1)S(1)} copy-done((bf16[1,256,4096]{2,1,0:T(8,128)(2,1)S(1)}, bf16[1,256,4096]{2,1,0:T(8,128)(2,1)}, u32[]{:S(2)}) %copy-start.1) | copy-done | bytes 2097176
  2.9 0.0 copy-start.2
  2.9 0.9 %copy-done.2 = bf16[1,256,512]{2,1,0:T(8,128)(2,1)S(1)} copy-done((bf16[1,256,512]{2,1,0:T(8,128)(2,1)S(1)}, bf16[1,256,512]{2,1,0:T(8,128)(2,1)}, u32[]{:S(2)}) %copy-start.2) | copy-done | bytes 262168
  3.9 0.0 copy-start.3
  3.9 0.9 %copy-done.3 = bf16[1,256,512]{2,1,0:T(8,128)(2,1)S(1)} copy-done((bf16[1,256,512]{2,1,0:T(8,128)(2,1)S(1)}, bf16[1,256,512]{2,1,0:T(8,128)(2,1)}, u32[]{:S(2)}) %copy-start.3) | copy-done | bytes 262168
  4.8 0.0 copy-start.4
  4.8 0.7 %copy-done.4 = f32[1,4096]{1,0:T(1,128)S(1)} copy-done((f32[1,4096]{1,0:T(1,128)S(1)}, f32[1,4096]{1,0:T(1,128)}, u32[]{:S(2)}) %copy-start.4) | copy-done | bytes 16408
  5.6 0.0 copy-start.5
  5.6 0.7 %copy-done.5 = s32[2048]{0:T(1024)S(1)} copy-done((s32[2048]{0:T(1024)S(1)}, s32[2048]{0:T(1024)}, u32[]{:S(2)}) %copy-start.5) | copy-done | bytes 8216
  6.3 47.7 %shard_map.77 = (bf16[256,4096]{1,0:T(8,128)(2,1)S(1)}, f32[256,128]{1,0:T(8,128)S(1)}, f32[1,256]{1,0:T(1,128)S(1)}) custom-call(bf16[1,256,4096]{2,1,0:T(8,128)(2,1)S(1)} %copy-done.1, bf16[1,256,512]{2,1,0:T(8,128)(2,1)S(1)} %copy-done.2, bf16[1,256,512]{2,1,0:T(8,128)(2,1)S(1)} %copy-done.3, s32[16,128]{1,0:T(8,128)S(1)} %bitcast.7, ...), custom_call_target="tpu_custom_call" | custom-call | flops 5368709120 | bytes 4194304 | tf_op jit(solution)/shard_map/pallas_call | solution.py:312
  54.0 0.1 slice_reduce_fusion
  54.1 2.0 %fusion = bf16[1,256,4096]{2,1,0:T(8,128)(2,1)} fusion(bf16[256,4096]{1,0:T(8,128)(2,1)S(1)} %get-tuple-element.5, f32[4096]{0:T(1024)S(1)} %bitcast.5, f32[256]{0:T(256)S(1)} %slice_reduce_fusion), kind=kLoop, calls=%fused_computation.1 | loop fusion | flops 4194304 | bytes 4211712 | tf_op jit(solution)/shard_map/broadcast_in_dim | solution.py:350
  56.1 0.6 copy.9
Async XLA Ops:
  0.6 0.7 %copy-start = (f32[1,4096]{1,0:T(1,128)S(1)}, f32[1,4096]{1,0:T(1,128)}, u32[]{:S(2)}) copy-start(f32[1,4096]{1,0:T(1,128)} %gain_ref.1) | copy-start | bytes 49156
  1.4 1.6 %copy-start.1 = (bf16[1,256,4096]{2,1,0:T(8,128)(2,1)S(1)}, bf16[1,256,4096]{2,1,0:T(8,128)(2,1)}, u32[]{:S(2)}) copy-start(bf16[1,256,4096]{2,1,0:T(8,128)(2,1)} %q_hbm.1) | copy-start | bytes 6291460
  2.9 0.9 %copy-start.2 = (bf16[1,256,512]{2,1,0:T(8,128)(2,1)S(1)}, bf16[1,256,512]{2,1,0:T(8,128)(2,1)}, u32[]{:S(2)}) copy-start(bf16[1,256,512]{2,1,0:T(8,128)(2,1)} %k_hbm.1) | copy-start | bytes 786436
  3.9 0.9 %copy-start.3 = (bf16[1,256,512]{2,1,0:T(8,128)(2,1)S(1)}, bf16[1,256,512]{2,1,0:T(8,128)(2,1)}, u32[]{:S(2)}) copy-start(bf16[1,256,512]{2,1,0:T(8,128)(2,1)} %v_hbm.1) | copy-start | bytes 786436
  4.8 0.7 %copy-start.4 = (f32[1,4096]{1,0:T(1,128)S(1)}, f32[1,4096]{1,0:T(1,128)}, u32[]{:S(2)}) copy-start(f32[1,4096]{1,0:T(1,128)} %weight_ref.1) | copy-start | bytes 49156
  5.6 0.7 %copy-start.5 = (s32[2048]{0:T(1024)S(1)}, s32[2048]{0:T(1024)}, u32[]{:S(2)}) copy-start(s32[2048]{0:T(1024)} %param.9) | copy-start | bytes 24580

commit v2 on v1

--- a/solution.py
+++ b/solution.py
@@ -19,10 +19,10 @@
 
 
 def kernel(
-    sizes, q_hbm, k_hbm, v_hbm, seg_ref, gain_ref, weight_ref,
+    sizes, q_hbm, k_hbm, v_hbm, seg_hbm, gain_hbm, weight_hbm,
     att_ref, inv_ref, joined_ref,
-    q_vm, kv, gmask, fmask, acc, best, squares, scored, stats,
-    q_sem, own_sem, col_send, col_recv, x_send, x_recv, st_send, st_recv,
+    q_vm, kv, vt, gmask, fmask, acc, best, squares, scored, stats, seg_ref, gain_ref, weight_ref,
+    q_sem, own_sem, row_sem, col_send, col_recv, x_send, x_recv, st_send, st_recv,
 ):
     n, branches, tps, span = sizes
     steps = span // 2
@@ -52,6 +52,14 @@
             )
     for copy in own:
         copy.start()
+    small = [
+        pltpu.make_async_copy(source, target, row_sem.at[number])
+        for number, (source, target) in enumerate(
+            ((seg_hbm, seg_ref), (gain_hbm, gain_ref), (weight_hbm, weight_ref))
+        )
+    ]
+    for copy in small:
+        copy.start()
     q_copy.start()
 
     peers = []
@@ -76,6 +84,8 @@
             barrier, inc=1, device_id={"branch": b_to, "tp": t_to}, device_id_type=MESH
         )
 
+    for copy in small:
+        copy.wait()
     lane = lax.broadcasted_iota(jnp.int32, (1, HD), 1)
     segs = seg_ref[...]
     total = segs.shape[0] * segs.shape[1]
@@ -94,6 +104,7 @@
     fmask[...] = ((member[span * rows :] - 1.0) * BIG).astype(jnp.bfloat16)
     squares[...] = jnp.zeros_like(squares)
     scored[...] = jnp.zeros_like(scored)
+    vt[:, HD:, :] = jnp.ones((groups, vt.shape[1] - HD, window), jnp.bfloat16)
 
     for distance in range(1, span + 1):
 
@@ -159,93 +170,116 @@
             def _():
                 x_copy(step - 1, g).start()
 
-    tri_row = lax.broadcasted_iota(jnp.int32, (2 * half, half), 0)
-    tri_col = lax.broadcasted_iota(jnp.int32, (2 * half, half), 1)
-    causal = tri_col <= lax.rem(tri_row, half)
-
-    def pair(step, g, index):
+    tri_key = lax.broadcasted_iota(jnp.int32, (half, 2 * half), 0)
+    tri_row = lax.broadcasted_iota(jnp.int32, (half, 2 * half), 1)
+    causal = tri_key <= lax.rem(tri_row, half)
+
+    def span_of(step, r):
+        first, last = (span - 2 * step) * rows, (span - 2 * step + 2) * rows
+        if step == 1:
+            last = span * rows + (r + 1) * half
+        if step == steps:
+            first += r * half
+        return first, last
+
+    def columns_of(g, index):
         top = g * per_group + 2 * index
-        for r in range(2):
-            lines = pl.ds(r * half, half)
-            first, last = (span - 2 * step) * rows, (span - 2 * step + 2) * rows
-            if step == 1:
-                last = span * rows + (r + 1) * half
-            if step == steps:
-                first += r * half
-            keys = pl.ds(first, last - first)
-            columns = [pl.ds(pl.multiple_of((top + e) * HD, HD), HD) for e in range(2)]
-            marks = fmask[lines, :]
-            left = jnp.concatenate(
-                [
-                    jnp.concatenate([q_vm[lines, columns[0]], q_vm[lines, columns[1]]], axis=0),
-                    jnp.concatenate([marks, marks], axis=0),
-                ],
-                axis=1,
+        return [pl.ds(pl.multiple_of((top + e) * HD, HD), HD) for e in range(2)]
+
+    def score(step, g, index, r):
+        first, last = span_of(step, r)
+        lines, keys = pl.ds(r * half, half), pl.ds(first, last - first)
+        columns = columns_of(g, index)
+        marks = fmask[lines, :]
+        query = jnp.concatenate(
+            [
+                jnp.concatenate([q_vm[lines, columns[0]], q_vm[lines, columns[1]]], axis=0),
+                jnp.concatenate([marks, marks], axis=0),
+            ],
+            axis=1,
+        )
+        key = jnp.concatenate([kv[g, 0, keys, :], gmask[keys, :]], axis=1)
+        scores = lax.dot_general(
+            key, query, (((1,), (1,)), ((), ())), preferred_element_type=jnp.float32
+        )
+        if step == 1:
+            body = last - first - half
+            scores = jnp.concatenate(
+                [scores[:body], jnp.where(causal, scores[body:], -BIG)], axis=0
             )
-            right = jnp.concatenate([kv[g, 0, keys, :], gmask[keys, :]], axis=1)
-            scores = lax.dot_general(
-                left, right, (((1,), (1,)), ((), ())), preferred_element_type=jnp.float32
-            )
-            if step == 1:
-                body = last - first - half
-                scores = jnp.concatenate(
-                    [scores[:, :body], jnp.where(causal, scores[:, body:], -BIG)], axis=1
-                )
-            peak = jnp.max(scores, axis=1, keepdims=True)
-            if step > 1:
-                before = best[top, lines, :], best[top + 1, lines, :]
-                before = jnp.concatenate(before, axis=0)
-                wide = jnp.maximum(before, peak)
-                peak = wide[:, :1]
-            weights = jnp.exp2((scores - peak) * scale).astype(jnp.bfloat16)
-            mixer = jnp.concatenate(
-                [kv[g, 1, keys, :], jnp.ones((last - first, HD), jnp.bfloat16)], axis=1
-            )
-            mixed = jnp.dot(weights, mixer, preferred_element_type=jnp.float32)
-            if step > 1:
-                shrink = jnp.exp2((before - wide) * scale)
-                earlier = jnp.concatenate(
-                    [acc[top, lines, :], acc[top + 1, lines, :]], axis=0
-                )
-                mixed = mixed + earlier * jnp.concatenate([shrink, shrink], axis=1)
-            if step < steps:
-                acc[top, lines, :] = mixed[:half]
-                acc[top + 1, lines, :] = mixed[half:]
-                wide = jnp.broadcast_to(peak, (2 * half, HD))
-                best[top, lines, :] = wide[:half]
-                best[top + 1, lines, :] = wide[half:]
-            else:
-                attended = (mixed[:, :HD] / mixed[:, HD:]).astype(jnp.bfloat16)
-                for e in range(2):
-                    out = attended[e * half : (e + 1) * half]
-                    att_ref[lines, columns[e]] = out
-                    out = out.astype(jnp.float32)
-                    line = gain_ref[:, columns[e]] * weight_ref[:, columns[e]]
-                    squares[lines, :] += out * out
-                    scored[lines, :] += out * line
-
-    units = [(step, g) for step in range(1, steps + 1) for g in range(groups)]
+        return scores
+
+    def mix(step, g, index, r, scores):
+        first, last = span_of(step, r)
+        lines = pl.ds(r * half, half)
+        unit = (g * (per_group // 2) + index) * 2 + r
+        peak = jnp.max(scores, axis=0, keepdims=True)
+        if step > 1:
+            before = best[unit, 0:1, :]
+            peak = jnp.maximum(before, peak)
+        weights = jnp.exp2((scores - peak) * scale).astype(jnp.bfloat16)
+        mixed = jnp.dot(
+            vt[g, :, pl.ds(first, last - first)], weights, preferred_element_type=jnp.float32
+        )
+        if step > 1:
+            mixed = mixed + acc[unit] * jnp.exp2((before - peak) * scale)
+        if step < steps:
+            acc[unit] = mixed
+            best[unit, 0:1, :] = peak
+            return
+        attended = mixed[:HD] * (1.0 / mixed[HD : HD + 1])
+        attended = attended.astype(jnp.bfloat16).astype(jnp.float32)
+        square = jnp.sum(attended * attended, axis=0, keepdims=True)
+        squares[0:1, lines] += square[:, :half] + square[:, half:]
+        turned = attended.T
+        columns = columns_of(g, index)
+        for e in range(2):
+            out = turned[e * half : (e + 1) * half]
+            att_ref[lines, columns[e]] = out.astype(jnp.bfloat16)
+            line = gain_ref[:, columns[e]] * weight_ref[:, columns[e]]
+            scored[lines, :] += out * line
+
     pairs = per_group // 2
-    arrive(*units[0])
+    arrive(1, 0)
     q_copy.wait()
-    for number, (step, g) in enumerate(units):
-
-        @pl.when(me >= 2 * step - 1)
-        def _(step=step, g=g):
-            x_copy(step - 1, g).wait_recv()
-
-        def walk(index, carry, step=step, g=g):
-            pair(step, g, index)
+    for step in range(1, steps + 1):
+
+        def group(g, carry, step=step):
+            @pl.when(me >= 2 * step - 1)
+            def _():
+                x_copy(step - 1, g).wait_recv()
+
+            keys = pl.ds((span - 2 * step) * rows, (2 + (step == 1)) * rows)
+            vt[g, pl.ds(0, HD), keys] = kv[g, 1, keys, :].astype(jnp.float32).T.astype(jnp.bfloat16)
+
+            def walk(part, inner):
+                chains = [(2 * part + more, r) for more in range(2) for r in range(2)]
+                scores = [score(step, g, *chains[0]), score(step, g, *chains[1])]
+                for number, chain in enumerate(chains):
+                    mix(step, g, *chain, scores[number])
+                    if number + 2 < len(chains):
+                        scores.append(score(step, g, *chains[number + 2]))
+
+                @pl.when((part == 0) & (g + 1 < groups))
+                def _():
+                    arrive(step, g + 1)
+
+                if step < steps:
+
+                    @pl.when((part == 0) & (g + 1 == groups))
+                    def _():
+                        arrive(step + 1, 0)
+
+                return inner
+
+            lax.fori_loop(0, pairs // 2, walk, 0)
             return carry
 
-        lax.fori_loop(0, pairs // 2, walk, 0)
-        if number + 1 < len(units):
-            arrive(*units[number + 1])
-        lax.fori_loop(pairs // 2, pairs, walk, 0)
+        lax.fori_loop(0, groups, group, 0)
 
     slab = jnp.concatenate(
         [
-            jnp.sum(squares[...].T, axis=0, keepdims=True),
+            squares[0:1, :],
             jnp.sum(scored[...].T, axis=0, keepdims=True),
             jnp.zeros((6, rows), jnp.float32),
         ],
@@ -307,7 +341,8 @@
     steps = span // 2
     devices = branches * tps
     vmem = pl.BlockSpec(memory_space=pltpu.VMEM)
-    hbm = pl.BlockSpec(memory_space=pl.ANY)
+    hbm = pl.BlockSpec(memory_space=pltpu.HBM)
+    seg_rows = segments.reshape(-1, HD)
     dma = pltpu.SemaphoreType.DMA
     attended, inverse, joined = pl.pallas_call(
         functools.partial(kernel, sizes),
@@ -316,20 +351,25 @@
             jax.ShapeDtypeStruct((rows, HD), jnp.float32),
             jax.ShapeDtypeStruct((1, rows), jnp.float32),
         ),
-        in_specs=[hbm, hbm, hbm, vmem, vmem, vmem],
+        in_specs=[hbm] * 6,
         out_specs=(vmem, vmem, vmem),
         scratch_shapes=[
             pltpu.VMEM((rows, columns), jnp.bfloat16),
             pltpu.VMEM((groups, 2, window, HD), jnp.bfloat16),
+            pltpu.VMEM((groups, HD + 16, window), jnp.bfloat16),
             pltpu.VMEM((window, HD), jnp.bfloat16),
             pltpu.VMEM((rows, HD), jnp.bfloat16),
-            pltpu.VMEM((heads, rows, 2 * HD), jnp.float32),
-            pltpu.VMEM((heads, rows, HD), jnp.float32),
-            pltpu.VMEM((rows, HD), jnp.float32),
+            pltpu.VMEM((heads, HD + 16, rows), jnp.float32),
+            pltpu.VMEM((heads, 8, rows), jnp.float32),
+            pltpu.VMEM((8, rows), jnp.float32),
             pltpu.VMEM((rows, HD), jnp.float32),
             pltpu.VMEM((devices, 8, rows), jnp.float32),
+            pltpu.VMEM(seg_rows.shape, jnp.int32),
+            pltpu.VMEM(norm_gain.shape, jnp.float32),
+            pltpu.VMEM(norm_gain.shape, jnp.float32),
             dma,
             dma((groups, 2)),
+            dma((3,)),
             dma((steps, groups)),
             dma((steps, groups)),
             dma((steps, groups)),
@@ -338,14 +378,14 @@
             dma((devices - 1,)),
         ],
         compiler_params=pltpu.CompilerParams(
-            collective_id=0, has_side_effects=True, vmem_limit_bytes=48 * 2**20
+            collective_id=0, has_side_effects=True, vmem_limit_bytes=60 * 2**20
         ),
         cost_estimate=pl.CostEstimate(
             flops=4 * rows * window * columns,
             bytes_accessed=4 * rows * columns,
             transcendentals=heads * rows * window,
         ),
-    )(queries, keys, values, segments.reshape(-1, HD), norm_gain, head_weight)
+    )(queries, keys, values, seg_rows, norm_gain, head_weight)
     normed = attended.astype(jnp.float32) * inverse[:, :1] * norm_gain
     return normed.astype(jnp.bfloat16)[None], joined.reshape(rows)
 

time: 57 us -> 45 us (0.79)
  Pallas kernels: 47.7 us -> 39 us
  local copies, waits for them, and re-layouts: 6.28 us -> 1.58 us
  other arithmetic: 1.97 us -> 3.54 us
    pallas_call x1, Pallas kernels: 47.7 us -> 39 us  [local(): pl.pallas_call(functools.partial(kernel, sizes), out_shape=(jax.ShapeDtyp...]
    unnamed x13 -> x5, local copies, waits for them, and re-layouts: 6.18 us -> 0.57 us
    broadcast_in_dim x1, other arithmetic: 1.97 us -> 3.54 us  [local(): return (normed.astype(jnp.bfloat16)[None], joined.reshape(rows))]
    slice x1, local copies, waits for them, and re-layouts: 0.1 us -> 1.01 us  [local(): normed = attended.astype(jnp.float32) * inverse[:, :1] * norm_gain]
where the time goes in v2:
time: 45 us; the launch traced here: 44.8 us
  Pallas kernels  39 us (87%)
  other arithmetic  3.54 us (8%)
  local copies, waits for them, and re-layouts  1.58 us (4%)
  between operations  0.67 us (1%)
    pallas_call x1, Pallas kernels, local(): pl.pallas_call(functools.partial(kernel, sizes), out_shape=(jax.ShapeDtyp...  39 us
    broadcast_in_dim x1, other arithmetic, local(): return (normed.astype(jnp.bfloat16)[None], joined.reshape(rows))  3.54 us
    slice x1, local copies, waits for them, and re-layouts, local(): normed = attended.astype(jnp.float32) * inverse[:, :1] * norm_gain  1.01 us

profile of v2, /device:TPU:25, one launch (start us, length us, event | category | flops | bytes accessed | tf_op | source)
XLA Modules:
  0.0 44.8 jit_solution(13924220749977729954)
XLA Ops:
  0.6 0.0 copy-start
  0.6 39.0 %shard_map.77 = (bf16[256,4096]{1,0:T(8,128)(2,1)}, f32[256,128]{1,0:T(8,128)}, f32[1,256]{1,0:T(1,128)}) custom-call(bf16[1,256,4096]{2,1,0:T(8,128)(2,1)} %q_hbm.1, bf16[1,256,512]{2,1,0:T(8,128)(2,1)} %k_hbm.1, bf16[1,256,512]{2,1,0:T(8,128)(2,1)} %v_hbm.1, s32[16,128]{1,0:T(8,128)} %bitcast.7, f32[1,4096]{1,0:T(1,128)} %gain_hbm.1, f32[1,4096]{1,0:T(1,128)} %weight_hbm.1), custom_call_target="tpu_custom_call" | custom-call | flops 5368709120 | bytes 4194304 | tf_op jit(solution)/shard_map/pallas_call | solution.py:347
  39.7 1.0 %slice_reduce_fusion = f32[256]{0:T(256)S(1)} fusion(f32[256,128]{1,0:T(8,128)} %get-tuple-element.6), kind=kLoop, calls=%fused_computation.2 | loop fusion | bytes 2048 | tf_op jit(solution)/shard_map/slice | solution.py:389
  40.7 0.0 copy-done
  40.7 0.0 copy-start.1
  40.7 3.5 %fusion = bf16[1,256,4096]{2,1,0:T(8,128)(2,1)} fusion(bf16[256,4096]{1,0:T(8,128)(2,1)} %get-tuple-element.5, f32[4096]{0:T(1024)S(1)} %bitcast.5, f32[256]{0:T(256)S(1)} %slice_reduce_fusion), kind=kLoop, calls=%fused_computation.1 | loop fusion | flops 4194304 | bytes 4211712 | tf_op jit(solution)/shard_map/broadcast_in_dim | solution.py:390
  44.2 0.0 copy-done.1
  44.2 0.6 %copy.9 = f32[256]{0:T(256)} copy(f32[256]{0:T(256)S(1)} %bitcast.6) | data formatting | bytes 2048
Async XLA Ops:
  0.6 40.0 %copy-start = (f32[1,4096]{1,0:T(1,128)S(1)}, f32[1,4096]{1,0:T(1,128)}, u32[]{:S(2)}) copy-start(f32[1,4096]{1,0:T(1,128)} %gain_hbm.1) | copy-start | bytes 49156
  40.7 3.6 %copy-start.1 = (f32[1,256]{1,0:T(1,128)S(1)}, f32[1,256]{1,0:T(1,128)}, u32[]{:S(2)}) copy-start(f32[1,256]{1,0:T(1,128)} %get-tuple-element.7) | copy-start | bytes 3076

commit v3 on v2

--- a/solution.py
+++ b/solution.py
@@ -253,22 +253,22 @@
             vt[g, pl.ds(0, HD), keys] = kv[g, 1, keys, :].astype(jnp.float32).T.astype(jnp.bfloat16)
 
             def walk(part, inner):
+                @pl.when((part == 0) & (g + 1 < groups))
+                def _():
+                    arrive(step, g + 1)
+
+                if step < steps:
+
+                    @pl.when((part == 0) & (g + 1 == groups))
+                    def _():
+                        arrive(step + 1, 0)
+
                 chains = [(2 * part + more, r) for more in range(2) for r in range(2)]
                 scores = [score(step, g, *chains[0]), score(step, g, *chains[1])]
                 for number, chain in enumerate(chains):
                     mix(step, g, *chain, scores[number])
                     if number + 2 < len(chains):
                         scores.append(score(step, g, *chains[number + 2]))
-
-                @pl.when((part == 0) & (g + 1 < groups))
-                def _():
-                    arrive(step, g + 1)
-
-                if step < steps:
-
-                    @pl.when((part == 0) & (g + 1 == groups))
-                    def _():
-                        arrive(step + 1, 0)
 
                 return inner
 

time: 45 us -> 45 us (level)
  no operation moved by 1% of the time
where the time goes in v3:
time: 45 us; the launch traced here: 44.8 us
  Pallas kernels  39 us (87%)
  other arithmetic  3.54 us (8%)
  local copies, waits for them, and re-layouts  1.58 us (4%)
  between operations  0.67 us (1%)
    pallas_call x1, Pallas kernels, local(): pl.pallas_call(functools.partial(kernel, sizes), out_shape=(jax.ShapeDtyp...  39 us
    broadcast_in_dim x1, other arithmetic, local(): return (normed.astype(jnp.bfloat16)[None], joined.reshape(rows))  3.54 us
    slice x1, local copies, waits for them, and re-layouts, local(): normed = attended.astype(jnp.float32) * inverse[:, :1] * norm_gain  1.01 us

profile of v3, /device:TPU:25, one launch (start us, length us, event | category | flops | bytes accessed | tf_op | source)
XLA Modules:
  0.0 44.8 jit_solution(4838123194729488868)
XLA Ops:
  0.6 0.0 copy-start
  0.6 39.0 %shard_map.77 = (bf16[256,4096]{1,0:T(8,128)(2,1)}, f32[256,128]{1,0:T(8,128)}, f32[1,256]{1,0:T(1,128)}) custom-call(bf16[1,256,4096]{2,1,0:T(8,128)(2,1)} %q_hbm.1, bf16[1,256,512]{2,1,0:T(8,128)(2,1)} %k_hbm.1, bf16[1,256,512]{2,1,0:T(8,128)(2,1)} %v_hbm.1, s32[16,128]{1,0:T(8,128)} %bitcast.7, f32[1,4096]{1,0:T(1,128)} %gain_hbm.1, f32[1,4096]{1,0:T(1,128)} %weight_hbm.1), custom_call_target="tpu_custom_call" | custom-call | flops 5368709120 | bytes 4194304 | tf_op jit(solution)/shard_map/pallas_call | solution.py:347
  39.6 1.0 %slice_reduce_fusion = f32[256]{0:T(256)S(1)} fusion(f32[256,128]{1,0:T(8,128)} %get-tuple-element.6), kind=kLoop, calls=%fused_computation.2 | loop fusion | bytes 2048 | tf_op jit(solution)/shard_map/slice | solution.py:389
  40.7 0.0 copy-done
  40.7 0.0 copy-start.1
  40.7 3.5 %fusion = bf16[1,256,4096]{2,1,0:T(8,128)(2,1)} fusion(bf16[256,4096]{1,0:T(8,128)(2,1)} %get-tuple-element.5, f32[4096]{0:T(1024)S(1)} %bitcast.5, f32[256]{0:T(256)S(1)} %slice_reduce_fusion), kind=kLoop, calls=%fused_computation.1 | loop fusion | flops 4194304 | bytes 4211712 | tf_op jit(solution)/shard_map/broadcast_in_dim | solution.py:390
  44.2 0.0 copy-done.1
  44.2 0.6 %copy.9 = f32[256]{0:T(256)} copy(f32[256]{0:T(256)S(1)} %bitcast.6) | data formatting | bytes 2048
Async XLA Ops:
  0.6 40.0 %copy-start = (f32[1,4096]{1,0:T(1,128)S(1)}, f32[1,4096]{1,0:T(1,128)}, u32[]{:S(2)}) copy-start(f32[1,4096]{1,0:T(1,128)} %gain_hbm.1) | copy-start | bytes 49156
  40.7 3.6 %copy-start.1 = (f32[1,256]{1,0:T(1,128)S(1)}, f32[1,256]{1,0:T(1,128)}, u32[]{:S(2)}) copy-start(f32[1,256]{1,0:T(1,128)} %get-tuple-element.7) | copy-start | bytes 3076

commit v4 on v3

--- a/solution.py
+++ b/solution.py
@@ -20,9 +20,9 @@
 
 def kernel(
     sizes, q_hbm, k_hbm, v_hbm, seg_hbm, gain_hbm, weight_hbm,
-    att_ref, inv_ref, joined_ref,
-    q_vm, kv, vt, gmask, fmask, acc, best, squares, scored, stats, seg_ref, gain_ref, weight_ref,
-    q_sem, own_sem, row_sem, col_send, col_recv, x_send, x_recv, st_send, st_recv,
+    att_out, inv_ref, joined_ref,
+    att_ref, q_vm, kv, vt, gmask, fmask, acc, best, squares, scored, stats, seg_ref, gain_ref, weight_ref,
+    q_sem, att_sem, own_sem, row_sem, col_send, col_recv, x_send, x_recv, st_send, st_recv,
 ):
     n, branches, tps, span = sizes
     steps = span // 2
@@ -239,6 +239,11 @@
             line = gain_ref[:, columns[e]] * weight_ref[:, columns[e]]
             scored[lines, :] += out * line
 
+    def att_copy(g):
+        wide = per_group * HD
+        columns = pl.ds(pl.multiple_of(g * wide, wide), wide)
+        return pltpu.make_async_copy(att_ref.at[:, columns], att_out.at[:, columns], att_sem.at[g])
+
     pairs = per_group // 2
     arrive(1, 0)
     q_copy.wait()
@@ -273,6 +278,8 @@
                 return inner
 
             lax.fori_loop(0, pairs // 2, walk, 0)
+            if step == steps:
+                att_copy(g).start()
             return carry
 
         lax.fori_loop(0, groups, group, 0)
@@ -314,6 +321,9 @@
 
     for number in range(len(peers)):
         stat_copy(number).wait()
+
+    for g in range(groups):
+        att_copy(g).wait()
 
     def inverse_of(branch):
         square_sum = stats[branch * tps, 0:1, :]
@@ -352,8 +362,9 @@
             jax.ShapeDtypeStruct((1, rows), jnp.float32),
         ),
         in_specs=[hbm] * 6,
-        out_specs=(vmem, vmem, vmem),
+        out_specs=(hbm, vmem, vmem),
         scratch_shapes=[
+            pltpu.VMEM((rows, columns), jnp.bfloat16),
             pltpu.VMEM((rows, columns), jnp.bfloat16),
             pltpu.VMEM((groups, 2, window, HD), jnp.bfloat16),
             pltpu.VMEM((groups, HD + 16, window), jnp.bfloat16),
@@ -368,6 +379,7 @@
             pltpu.VMEM(norm_gain.shape, jnp.float32),
             pltpu.VMEM(norm_gain.shape, jnp.float32),
             dma,
+            dma((groups,)),
             dma((groups, 2)),
             dma((3,)),
             dma((steps, groups)),

time: 45 us -> 44.4 us (0.987)
  Pallas kernels: 39 us -> 38.4 us
    pallas_call x1, Pallas kernels: 39 us -> 38.4 us  [local(): pl.pallas_call(functools.partial(kernel, sizes), out_shape=(jax.ShapeDtyp...]
where the time goes in v4:
time: 44.4 us; the launch traced here: 44.2 us
  Pallas kernels  38.4 us (86%)
  other arithmetic  3.54 us (8%)
  local copies, waits for them, and re-layouts  1.58 us (4%)
  between operations  0.67 us (2%)
    pallas_call x1, Pallas kernels, local(): pl.pallas_call(functools.partial(kernel, sizes), out_shape=(jax.ShapeDtyp...  38.4 us
    broadcast_in_dim x1, other arithmetic, local(): return (normed.astype(jnp.bfloat16)[None], joined.reshape(rows))  3.54 us
    slice x1, local copies, waits for them, and re-layouts, local(): normed = attended.astype(jnp.float32) * inverse[:, :1] * norm_gain  1.01 us

profile of v4, /device:TPU:25, one launch (start us, length us, event | category | flops | bytes accessed | tf_op | source)
XLA Modules:
  0.0 44.2 jit_solution(566933753773773292)
XLA Ops:
  0.6 0.0 copy-start
  0.6 38.4 %shard_map.77 = (bf16[256,4096]{1,0:T(8,128)(2,1)}, f32[256,128]{1,0:T(8,128)}, f32[1,256]{1,0:T(1,128)}) custom-call(bf16[1,256,4096]{2,1,0:T(8,128)(2,1)} %q_hbm.1, bf16[1,256,512]{2,1,0:T(8,128)(2,1)} %k_hbm.1, bf16[1,256,512]{2,1,0:T(8,128)(2,1)} %v_hbm.1, s32[16,128]{1,0:T(8,128)} %bitcast.7, f32[1,4096]{1,0:T(1,128)} %gain_hbm.1, f32[1,4096]{1,0:T(1,128)} %weight_hbm.1), custom_call_target="tpu_custom_call" | custom-call | flops 5368709120 | bytes 4194304 | tf_op jit(solution)/shard_map/pallas_call | solution.py:357
  39.1 1.0 %slice_reduce_fusion = f32[256]{0:T(256)S(1)} fusion(f32[256,128]{1,0:T(8,128)} %get-tuple-element.6), kind=kLoop, calls=%fused_computation.2 | loop fusion | bytes 2048 | tf_op jit(solution)/shard_map/slice | solution.py:401
  40.1 0.0 copy-done
  40.1 0.0 copy-start.1
  40.1 3.5 %fusion = bf16[1,256,4096]{2,1,0:T(8,128)(2,1)} fusion(bf16[256,4096]{1,0:T(8,128)(2,1)} %get-tuple-element.5, f32[4096]{0:T(1024)S(1)} %bitcast.5, f32[256]{0:T(256)S(1)} %slice_reduce_fusion), kind=kLoop, calls=%fused_computation.1 | loop fusion | flops 4194304 | bytes 4211712 | tf_op jit(solution)/shard_map/broadcast_in_dim | solution.py:402
  43.6 0.0 copy-done.1
  43.7 0.6 %copy.9 = f32[256]{0:T(256)} copy(f32[256]{0:T(256)S(1)} %bitcast.6) | data formatting | bytes 2048
Async XLA Ops:
  0.6 39.5 %copy-start = (f32[1,4096]{1,0:T(1,128)S(1)}, f32[1,4096]{1,0:T(1,128)}, u32[]{:S(2)}) copy-start(f32[1,4096]{1,0:T(1,128)} %gain_hbm.1) | copy-start | bytes 49156
  40.1 3.6 %copy-start.1 = (f32[1,256]{1,0:T(1,128)S(1)}, f32[1,256]{1,0:T(1,128)}, u32[]{:S(2)}) copy-start(f32[1,256]{1,0:T(1,128)} %get-tuple-element.7) | copy-start | bytes 3076
